TPU v7x, 32 devices: a whole 2x2x4 slice. The times are simulated.
32 devices in a mesh: tower: 2 (over core), rows: 16 (over z, y, x).
Axes of the slice: x: 2, y: 2, z: 4, core: 2. Of those that a mesh axis runs over, the one named last changes fastest.
Arguments:
- tokens: bfloat16 [2, 32, 512, 512], P('tower', 'rows'), may hold values from -9 to 9
- segment_ids: int32 [2, 32, 512], P('tower', 'rows'), may hold values from 0 to 8, never falling along the last dimension, each value on 1 to 128 neighbouring positions
- positives: int32 [256], P('rows'), may hold values from 0 to 255, each once
- attention_gain: float32 [512], replicated, may hold values from 0.5 to 1.5
- query_weight: bfloat16 [512, 512], replicated, may hold values from -0.0625 to 0.0625
- key_weight: bfloat16 [512, 512], replicated, may hold values from -0.25 to 0.25
- value_weight: bfloat16 [512, 512], replicated, may hold values from -0.25 to 0.25
- output_weight: bfloat16 [512, 512], replicated, may hold values from -1 to 1
- position_table: float32 [32, 8], replicated, may hold values from -3 to 3
- feedforward_gain: float32 [512], replicated, may hold values from 0.5 to 1.5
- inner_weight: bfloat16 [512, 2048], replicated, may hold values from -0.25 to 0.25
- outer_weight: bfloat16 [2048, 512], replicated, may hold values from -0.1875 to 0.1875
Outputs:
- layer_output: bfloat16 [2, 32, 512, 512], P('tower', 'rows')
- token_grad: bfloat16 [2, 32, 512, 512], P('tower', 'rows')
- attention_gain_grad: float32 [512], replicated
- query_grad: float32 [512, 512], replicated
- key_grad: float32 [512, 512], replicated
- value_grad: float32 [512, 512], replicated
- output_grad: float32 [512, 512], replicated
- position_grad: float32 [32, 8], replicated
- feedforward_gain_grad: float32 [512], replicated
- inner_grad: float32 [512, 2048], replicated
- outer_grad: float32 [2048, 512], replicated
- contrastive_loss: float32 [], replicated
- root_mean_squares: float32 [3], replicated
Inputs may be any that keep to these rules, and one draw needn't show every extreme that they name: `segment_ids`: within each row of 512 tokens the numbers never fall; 0 to 7 are the row's items and 8 marks the padding at its end; every number, padding included, covers 1 to 128 tokens. positives[m] is the document item paired with query item m; every document item occurs once.
All inputs are finite; a program needn't handle non-finite values.
Results may differ from a plain program's by a relative error of at most 0.028.
The roundings to bfloat16 on the way count: a program that leaves them out, or rounds other values in their place, can miss the bound.
Values sent between devices are 32-bit elements; how exact they have to be, the bound alone decides.
A program may use at most 320 MiB of HBM per device.

v0:
```python
import math
import jax
import jax.numpy as jnp
import numpy as np
from jax import lax
from jax.sharding import PartitionSpec as P

MAX_DIST = 128
ITEMS_ROW = 8
EPSILON = 1e-06
SOFTMAX_TEMP = 0.01
LOSS_SCALE = 65536.0
MATMUL_PRECISION = lax.Precision.HIGHEST


def from_partner(value, axis, apart):
    mask = 2**apart
    pairs = [(source, source ^ mask) for source in range(lax.axis_size(axis))]
    return lax.ppermute(value, axis, pairs)


def bucket_table(length, bucket_count, far_limit):
    half_count = bucket_count // 2
    exact_count = half_count // 2
    entries = []
    for offset in range(1 - length, length):
        distance = abs(offset)
        if distance < exact_count:
            within = distance
        else:
            within = exact_count + int(
                math.log(distance / exact_count)
                / math.log(far_limit / exact_count)
                * (half_count - exact_count)
            )
            within = min(within, half_count - 1)
        entries.append(within + (half_count if offset > 0 else 0))
    by_offset = np.array(entries, dtype=np.int32)
    index_grid = np.arange(length)[None, :] - np.arange(length)[:, None] + length - 1
    return (by_offset, by_offset[index_grid])


def contract_rows(left_side, right_side):
    return lax.dot_general(
        left_side, right_side, (((0,), (0,)), ((), ())), preferred_element_type=jnp.float32
    )


def times_transpose(left_side, right_side):
    return lax.dot_general(
        left_side, right_side, (((1,), (1,)), ((), ())), preferred_element_type=jnp.float32
    )


def norm_scale(values):
    return lax.rsqrt(jnp.mean(values * values, axis=1, keepdims=True) + EPSILON)


def norm_back(grad_normed, values, scale, gain):
    gained = grad_normed * gain
    return scale * (
        gained - values * scale * scale * jnp.mean(gained * values, axis=1, keepdims=True)
    )


def row_scores(query_part, key_part, segment_row, position_bias, head_count):
    length = query_part.shape[0]
    query_heads = query_part.reshape(length, head_count, -1)
    key_heads = key_part.reshape(length, head_count, -1)
    scores = (
        jnp.einsum("qhd,khd->hqk", query_heads, key_heads, preferred_element_type=jnp.float32)
        + position_bias
    )
    same_item = segment_row[:, None] == segment_row[None, :]
    return jnp.where(same_item[None], scores, -1e30)


def diagonal_sums(square):
    head_count = square.shape[0]
    length = square.shape[1]
    flipped = square[:, :, ::-1]
    padded = jnp.pad(flipped, ((0, 0), (0, 0), (0, length)))
    sheared = padded.reshape(head_count, 2 * length * length)[:, : length * (2 * length - 1)]
    sheared = sheared.reshape(head_count, length, 2 * length - 1)
    return jnp.sum(sheared, axis=1)[:, ::-1]


def shards(
    tokens,
    segment_ids,
    positives,
    attention_gain,
    query_weight,
    key_weight,
    value_weight,
    output_weight,
    position_table,
    feedforward_gain,
    inner_weight,
    outer_weight,
):
    row_count = tokens.shape[1]
    length = tokens.shape[2]
    model_width = tokens.shape[3]
    head_count = position_table.shape[1]
    inner_width = query_weight.shape[1]
    head_size = inner_width // head_count
    token_count = row_count * length
    by_offset, bucket_index = bucket_table(length, position_table.shape[0], MAX_DIST)
    position_bias = jnp.take(position_table.T, jnp.asarray(bucket_index), axis=1)
    inputs = tokens.reshape(token_count, model_width).astype(jnp.float32)
    segments = segment_ids.reshape(row_count, length)
    scale_one = norm_scale(inputs)
    normed_one = (inputs * scale_one * attention_gain).astype(jnp.bfloat16)
    query_rows = jnp.dot(normed_one, query_weight, preferred_element_type=jnp.float32).astype(
        jnp.bfloat16
    )
    key_rows = jnp.dot(normed_one, key_weight, preferred_element_type=jnp.float32).astype(
        jnp.bfloat16
    )
    value_rows = jnp.dot(normed_one, value_weight, preferred_element_type=jnp.float32).astype(
        jnp.bfloat16
    )
    query_blocks = query_rows.reshape(row_count, length, inner_width)
    key_blocks = key_rows.reshape(row_count, length, inner_width)
    value_blocks = value_rows.reshape(row_count, length, inner_width)

    def attend(packed):
        query_part, key_part, value_part, segment_row = packed
        scores = row_scores(query_part, key_part, segment_row, position_bias, head_count)
        highest = jnp.max(scores, axis=2, keepdims=True)
        exp_scores = jnp.exp(scores - highest)
        exp_total = jnp.sum(exp_scores, axis=2, keepdims=True)
        attention_probs = (exp_scores / exp_total).astype(jnp.bfloat16)
        value_heads = value_part.reshape(length, head_count, head_size)
        mixed_heads = jnp.einsum(
            "hqk,khd->qhd", attention_probs, value_heads, preferred_element_type=jnp.float32
        )
        return (
            mixed_heads.reshape(length, inner_width).astype(jnp.bfloat16),
            (highest + jnp.log(exp_total))[:, :, 0],
        )

    mixed_blocks, log_totals = lax.map(attend, (query_blocks, key_blocks, value_blocks, segments))
    mixed_rows = mixed_blocks.reshape(token_count, inner_width)
    branch_one = jnp.dot(mixed_rows, output_weight, preferred_element_type=jnp.float32)
    middle = inputs + branch_one
    scale_two = norm_scale(middle)
    normed_two = (middle * scale_two * feedforward_gain).astype(jnp.bfloat16)
    hidden = jax.nn.relu(
        jnp.dot(normed_two, inner_weight, preferred_element_type=jnp.float32)
    ).astype(jnp.bfloat16)
    branch_two = jnp.dot(hidden, outer_weight, preferred_element_type=jnp.float32)
    result = middle + branch_two
    valid_mask = (segments < ITEMS_ROW).astype(jnp.float32).reshape(token_count, 1)
    stat_terms = jnp.stack(
        [
            jnp.sum(valid_mask * result * result),
            jnp.sum(valid_mask * branch_one * branch_one),
            jnp.sum(valid_mask * branch_two * branch_two),
            jnp.sum(valid_mask),
        ]
    )
    stat_totals = lax.psum(stat_terms, ("tower", "rows"))
    member = (segments[:, None, :] == jnp.arange(ITEMS_ROW)[None, :, None]).astype(jnp.float32)
    item_sizes = jnp.sum(member, axis=2, keepdims=True)
    result_blocks = result.reshape(row_count, length, model_width)
    pooled = (
        jnp.einsum("ris,rsd->rid", member, result_blocks, precision=MATMUL_PRECISION) / item_sizes
    )
    items_here = row_count * ITEMS_ROW
    pooled = pooled.reshape(items_here, model_width)
    inverse_norm = lax.rsqrt(jnp.sum(pooled * pooled, axis=1, keepdims=True) + EPSILON)
    embedded_tokens = pooled * inverse_norm
    tower_index = lax.axis_index("tower")
    is_query = tower_index == 0
    partner = from_partner(embedded_tokens, "tower", 0)
    query_vectors = jnp.where(is_query, embedded_tokens, partner)
    document_vectors = jnp.where(is_query, partner, embedded_tokens)
    gathered_documents = lax.all_gather(document_vectors, "rows", axis=0, tiled=True)
    item_total = gathered_documents.shape[0]
    half_items = items_here // 2
    my_queries = lax.dynamic_slice_in_dim(query_vectors, tower_index * half_items, half_items, 0)
    my_targets = lax.dynamic_slice_in_dim(positives, tower_index * half_items, half_items, 0)
    similarity_scores = (
        lax.dot_general(
            my_queries,
            gathered_documents,
            (((1,), (1,)), ((), ())),
            precision=MATMUL_PRECISION,
            preferred_element_type=jnp.float32,
        )
        / SOFTMAX_TEMP
    )
    highest = jnp.max(similarity_scores, axis=1, keepdims=True)
    exp_logits = jnp.exp(similarity_scores - highest)
    exp_total = jnp.sum(exp_logits, axis=1, keepdims=True)
    log_total = highest[:, 0] + jnp.log(exp_total[:, 0])
    is_target = jnp.arange(item_total)[None, :] == my_targets[:, None]
    target = jnp.sum(jnp.where(is_target, similarity_scores, 0.0), axis=1)
    loss_part = jnp.sum(log_total - target)
    similarity_gradient = (exp_logits / exp_total - is_target.astype(jnp.float32)) * (
        LOSS_SCALE / item_total
    )
    local_gradient = (
        jnp.dot(similarity_gradient, gathered_documents, precision=MATMUL_PRECISION) / SOFTMAX_TEMP
    )
    grad_documents = lax.psum_scatter(
        lax.dot_general(
            similarity_gradient,
            my_queries,
            (((0,), (0,)), ((), ())),
            precision=MATMUL_PRECISION,
            preferred_element_type=jnp.float32,
        )
        / SOFTMAX_TEMP,
        "rows",
        scatter_dimension=0,
        tiled=True,
    )
    partner_mine, partner_documents = from_partner((local_gradient, grad_documents), "tower", 0)
    query_side = jnp.where(
        is_query,
        jnp.concatenate([local_gradient, partner_mine], 0),
        jnp.concatenate([partner_mine, local_gradient], 0),
    )
    own_grad = jnp.where(is_query, query_side, grad_documents + partner_documents)
    inner_along = jnp.sum(own_grad * embedded_tokens, axis=1, keepdims=True)
    grad_pooled = inverse_norm * (own_grad - embedded_tokens * inner_along)
    per_token = grad_pooled.reshape(row_count, ITEMS_ROW, model_width) / item_sizes
    grad_result = jnp.einsum("ris,rid->rsd", member, per_token, precision=MATMUL_PRECISION).reshape(
        token_count, model_width
    )
    grad_branch_two = grad_result.astype(jnp.bfloat16)
    outer_grad = contract_rows(hidden, grad_branch_two)
    grad_hidden = times_transpose(grad_branch_two, outer_weight)
    grad_pre = jnp.where(hidden > 0, grad_hidden, 0.0).astype(jnp.bfloat16)
    inner_grad = contract_rows(normed_two, grad_pre)
    grad_normed_two = times_transpose(grad_pre, inner_weight)
    feedforward_gain_grad = jnp.sum(grad_normed_two * middle * scale_two, axis=0)
    grad_middle = grad_result + norm_back(grad_normed_two, middle, scale_two, feedforward_gain)
    grad_branch_one = grad_middle.astype(jnp.bfloat16)
    output_grad = contract_rows(mixed_rows, grad_branch_one)
    grad_mixed = times_transpose(grad_branch_one, output_weight).astype(jnp.bfloat16)
    grad_mixed_blocks = grad_mixed.reshape(row_count, length, inner_width)

    def attend_back(running, packed):
        query_part, key_part, value_part, segment_row, row_log_total, grad_part = packed
        scores = row_scores(query_part, key_part, segment_row, position_bias, head_count)
        attention_probs = jnp.exp(scores - row_log_total[:, :, None])
        query_heads = query_part.reshape(length, head_count, head_size)
        key_heads = key_part.reshape(length, head_count, head_size)
        value_heads = value_part.reshape(length, head_count, head_size)
        grad_heads = grad_part.reshape(length, head_count, head_size)
        grad_value = jnp.einsum(
            "hqk,qhd->khd",
            attention_probs.astype(jnp.bfloat16),
            grad_heads,
            preferred_element_type=jnp.float32,
        )
        grad_probs = jnp.einsum(
            "qhd,khd->hqk", grad_heads, value_heads, preferred_element_type=jnp.float32
        )
        row_dot = jnp.sum(attention_probs * grad_probs, axis=2, keepdims=True)
        grad_scores = (attention_probs * (grad_probs - row_dot)).astype(jnp.bfloat16)
        grad_query = jnp.einsum(
            "hqk,khd->qhd", grad_scores, key_heads, preferred_element_type=jnp.float32
        )
        grad_key = jnp.einsum(
            "hqk,qhd->khd", grad_scores, query_heads, preferred_element_type=jnp.float32
        )
        outputs = (
            grad_query.reshape(length, inner_width).astype(jnp.bfloat16),
            grad_key.reshape(length, inner_width).astype(jnp.bfloat16),
            grad_value.reshape(length, inner_width).astype(jnp.bfloat16),
        )
        return (running + grad_scores.astype(jnp.float32), outputs)

    score_sum, grad_rows = lax.scan(
        attend_back,
        jnp.zeros((head_count, length, length), jnp.float32),
        (query_blocks, key_blocks, value_blocks, segments, log_totals, grad_mixed_blocks),
    )
    grad_queries = grad_rows[0].reshape(token_count, inner_width)
    grad_keys = grad_rows[1].reshape(token_count, inner_width)
    grad_values = grad_rows[2].reshape(token_count, inner_width)
    query_grad = contract_rows(normed_one, grad_queries)
    key_grad = contract_rows(normed_one, grad_keys)
    value_grad = contract_rows(normed_one, grad_values)
    grad_normed_one = (
        times_transpose(grad_queries, query_weight)
        + times_transpose(grad_keys, key_weight)
        + times_transpose(grad_values, value_weight)
    )
    attention_gain_grad = jnp.sum(grad_normed_one * inputs * scale_one, axis=0)
    token_grad = grad_middle + norm_back(grad_normed_one, inputs, scale_one, attention_gain)
    offset_onehot = jnp.asarray(
        (by_offset[:, None] == np.arange(position_table.shape[0])[None, :]).astype(np.float32)
    )
    position_grad = jnp.dot(diagonal_sums(score_sum), offset_onehot, precision=MATMUL_PRECISION).T
    closing_terms = loss_part[None]
    summed = lax.psum(
        (
            attention_gain_grad,
            query_grad,
            key_grad,
            value_grad,
            output_grad,
            position_grad,
            feedforward_gain_grad,
            inner_grad,
            outer_grad,
            closing_terms,
        ),
        ("tower", "rows"),
    )
    (
        attention_gain_grad,
        query_grad,
        key_grad,
        value_grad,
        output_grad,
        position_grad,
        feedforward_gain_grad,
        inner_grad,
        outer_grad,
        closing_totals,
    ) = summed
    contrastive_loss = closing_totals[0] / item_total
    root_mean_squares = jnp.sqrt(stat_totals[:3] / (stat_totals[3] * model_width))
    block_shape = (1, row_count, length, model_width)
    return (
        result.reshape(block_shape).astype(jnp.bfloat16),
        token_grad.reshape(block_shape).astype(jnp.bfloat16),
        attention_gain_grad,
        query_grad,
        key_grad,
        value_grad,
        output_grad,
        position_grad,
        feedforward_gain_grad,
        inner_grad,
        outer_grad,
        contrastive_loss,
        root_mean_squares,
    )


def solution(mesh):
    return jax.shard_map(
        shards,
        mesh=mesh,
        in_specs=(
            P("tower", "rows", None, None),
            P("tower", "rows", None),
            P("rows"),
            P(),
            P(),
            P(),
            P(),
            P(),
            P(),
            P(),
            P(),
            P(),
        ),
        out_specs=(
            P("tower", "rows", None, None),
            P("tower", "rows", None, None),
            P(),
            P(),
            P(),
            P(),
            P(),
            P(),
            P(),
            P(),
            P(),
            P(),
            P(),
        ),
        check_vma=False,
    )
```

profile of v0, /device:TPU:0, one launch (start us, length us, event | category | flops | bytes accessed | tf_op | source)
XLA Modules:
  0.0 1486.5 jit_solution(8252469070416313084)
XLA Ops:
  26.5 865.7 %gather_fusion = f32[262144,8]{1,0:T(8,128)} fusion(f32[8,32]{0,1:T(8,128)S(1)} %bitcast.203, s32[262144]{0:T(1024)S(1)} %broadcast_clamp_fusion), kind=kCustom, calls=%fused_computation | custom fusion | bytes 17825792 | tf_op jit(solution)/shard_map/jit(_take)/gather | solution.py:110
  892.2 70.9 %copy.45 = f32[512,512,8]{0,1,2:T(8,128)} copy(f32[512,512,8]{2,1,0:T(8,128)} %bitcast.13) | data formatting | bytes 16777216 | tf_op jit(solution)/shard_map/jit(_take)/gather | solution.py:110
  964.2 22.9 %while.29 = (s32[]{:T(128)}, bf16[2,512,512]{2,1,0:T(8,128)(2,1)}, f32[2,8,512]{2,1,0:T(8,128)S(1)}, bf16[2,512,512]{1,2,0:T(8,128)(2,1)}, s32[2,512]{1,0:T(2,12...) while((s32[]{:T(128)}, bf16[2,512,512]{2,1,0:T(8,128)(2,1)}, ...), condition=%wide.region_4.5_spmd, body=%wide.region_1.0_spmd.sunk | while | flops 554168320 | bytes 41556588 | solution.py:144
  965.7 5.0 fusion.126
  977.1 5.0 fusion.126
  999.4 45.4 %all_gather.3 = f32[256,512]{1,0:T(8,128)S(1)} all-gather(f32[16,512]{1,0:T(8,128)S(1)} %broadcast_select_fusion), channel_id=1, replica_groups=mesh['tower'=2,'rows'=16] {'rows'}, dimensions={0}, use_global_device_ids=true | all-gather | bytes 557056 | tf_op jit(solution)/shard_map/all_gather | solution.py:180
  1050.2 70.9 %reduce-scatter.2.cloned.1.call-done = f32[16,512]{1,0:T(8,128)} async-done(((f32[256,512]{1,0:T(8,128)}), f32[16,512]{1,0:T(8,128)}) %reduce-scatter.2.cloned.1.call-update) | async-done | bytes 32784 | tf_op jit(solution)/shard_map/reduce_scatter | solution.py:208
  1150.7 74.2 %while.30 = (s32[]{:T(128)}, f32[8,512,512]{1,2,0:T(8,128)}, bf16[2,512,512]{2,1,0:T(8,128)(2,1)}, bf16[2,512,512]{2,1,0:T(8,128)(2,1)}, bf16[2,512,512]{2,1,0:T...) while((s32[]{:T(128)}, f32[8,512,512]{1,2,0:T(8,128)}, ...), condition=%wide.region_15.16_spmd.clone, body=%wide.region_13.15_spmd.clone.sunk | while | flops 1368387584 | bytes 197745472 | solution.py:279
  1159.0 5.0 multiply_reduce_fusion.7
  1164.0 9.8 select_add_fusion.2
  1175.9 4.8 fusion.140
  1194.5 5.0 multiply_reduce_fusion.7
  1199.5 13.0 select_add_fusion.2
  1214.6 4.8 fusion.140
  1238.3 64.2 %rev.6 = f32[8,512,512]{1,2,0:T(8,128)} reverse(f32[8,512,512]{1,2,0:T(8,128)} %get-tuple-element.126), dimensions={2} | reverse | bytes 16777216 | tf_op jit(solution)/shard_map/rev | solution.py:81
  1302.6 9.6 copy.71
  1312.2 11.6 pad_bitcast_fusion
  1323.9 15.4 %copy.73 = f32[1,8,512,1024]{3,1,2,0:T(8,128)S(1)} copy(f32[1,8,512,1024]{3,2,1,0:T(8,128)} %pad_bitcast_fusion) | data formatting | bytes 33554432
  1339.3 6.0 slice.14
  1345.3 13.0 reshape.408
  1358.2 17.5 %reshape.392 = f32[8,512,1023]{2,1,0:T(8,128)} reshape(f32[4190208]{0:T(1024)} %reshape.408) | data formatting | bytes 33521664 | tf_op jit(solution)/shard_map/reshape | solution.py:84
  1375.8 7.4 reduce_sum.180
  1389.2 37.9 %all-reduce.1 = (f32[512]{0:T(512)}, f32[32,8]{0,1:T(8,128)}, f32[512]{0:T(512)}, f32[1]{0:T(128)}, f32[4]{0:T(128)S(1)}) all-reduce(f32[512]{0:T(512)S(1)} %get-tuple-element.208, f32[32,8]{0,1:T(8,128)S(1)} %fusion.48, f32[512]{0:T(512)S(1)} %copy-done.46, f32[1]{0:T(128)} %bitcast.27, ...), channel_id=1, replica_groups=mesh['tower'=2,'rows'=16] {'tower','rows'}, use_global_device_ids=true, to_apply=%region_18.19 | all-reduce | flops 1285 | bytes 10280 | tf_op jit(solution)/shard_map/psum | solution.py:302
  1433.6 32.4 %all-reduce.5.cloned.1.call-done = (f32[512,512]{1,0:T(8,128)}, f32[512,512]{1,0:T(8,128)}, f32[512,512]{1,0:T(8,128)}, f32[512,512]{1,0:T(8,128)}, f32[512,2048]{1,0:T(8,128)}, /*index=5*/f32[2048,512]{1,0:T(8,128)}) async-done(((f32[512,512]{1,0:T(8,128)}, f32[512,512]{1,0:T(8,128)}, f32[512,512]{1,0:T(8,128)}, f32[512,512]{1,0:T(8,128)}, f32[512,2048]{1,0:T(8,128)}, /*index=5*/f32[2048,512]{1,0:T(8,128)}), ...) | async-done | bytes 12582928 | tf_op jit(solution)/shard_map/psum | solution.py:302
  (243 shorter events, 148.7 us)
Async XLA Ops:
  7.2 982.5 %copy-start = (bf16[512,2048]{1,0:T(8,128)(2,1)S(1)}, bf16[512,2048]{1,0:T(8,128)(2,1)}, u32[]{:S(2)}) copy-start(bf16[512,2048]{1,0:T(8,128)(2,1)} %param.28) | copy-start | bytes 6291460
  7.2 1114.0 %reduce-scatter.2.cloned.1.call-start = ((), (), s32[]{:S(2)}) async-start(), calls=%async_computation.1 | async-start | bytes 557056 | tf_op jit(solution)/shard_map/reduce_scatter | solution.py:208
  892.2 70.9 %copy-start.32 = (s32[1,2,512]{2,1,0:T(2,128)S(1)}, s32[1,2,512]{2,1,0:T(2,128)}, u32[]{:S(2)}) copy-start(s32[1,2,512]{2,1,0:T(2,128)} %param.19) | copy-start | bytes 12292
  996.9 124.2 %copy-start.5 = (bf16[1,2,512,512]{3,2,1,0:T(8,128)(2,1)S(1)}, bf16[1,2,512,512]{3,2,1,0:T(8,128)(2,1)}, u32[]{:S(2)}) copy-start(bf16[1,2,512,512]{3,2,1,0:T(8,128)(2,1)} %param.18) | copy-start | bytes 3145732
  996.9 124.2 %copy-start.35 = (f32[512]{0:T(512)S(1)}, f32[512]{0:T(512)}, u32[]{:S(2)}) copy-start(f32[512]{0:T(512)} %param.21) | copy-start | bytes 6148
  996.9 124.2 %copy-start.39 = (f32[2,512]{1,0:T(2,128)S(1)}, f32[2,512]{1,0:T(2,128)}, u32[]{:S(2)}) copy-start(f32[2,512]{1,0:T(2,128)} %get-tuple-element.281) | copy-start | bytes 12292
  998.0 1.3 collective-permute-start
  1046.2 4.0 copy-start.40
  1048.5 417.5 %all-reduce.5.cloned.1.call-start = ((), (), s32[]{:S(2)}) async-start(), calls=%async_computation.2 | async-start | bytes 25165824 | tf_op jit(solution)/shard_map/psum | solution.py:302
  1050.2 72.2 %collective-permute-start.1 = (f32[8,512]{1,0:T(8,128)S(1)}, f32[8,512]{1,0:T(8,128)S(1)}, u32[]{:S(2)}, u32[]{:S(2)}) collective-permute-start(f32[8,512]{1,0:T(8,128)S(1)} %convolution_multiply_fusion.1), channel_id=1, source_target_pairs={{0,16},{16,0},{1,17},{17,1},{2,18},{18,2},{3,19},{19,3},{4,20},{20... | collective-permute-start | bytes 49160 | tf_op jit(solution)/shard_map/ppermute | solution.py:19
  1121.2 1.4 collective-permute-start.2
  1125.4 4.7 copy-start.51
  1130.1 4.5 copy-start.9
  1152.0 6.9 copy-start.3
  1153.4 10.6 copy-start.2
  1187.6 6.9 copy-start.3
  1188.9 10.6 copy-start.2
  1233.4 4.4 copy-start.41
  1233.4 4.4 copy-start.43
  1233.4 4.4 copy-start.45
  1375.8 8.0 copy-start.31
  1375.8 8.4 copy-start.16
  1375.8 8.4 copy-start.27
  1466.1 4.4 copy-start.24
  (38 other events, 89.4 us)
Sparse Core Ops, SparseCore 0:
  1048.7 72.4 reduce-scatter.1
  1231.9 234.1 all-reduce.4
where the time goes:
time: 1500 us; the launch traced here: 1490 us
  local copies, waits for them, and re-layouts  1130 us (75%)
  waiting for transfers between devices  104 us (7%)
  matrix products  95.6 us (6%)
  blocking collectives  83.3 us (6%)
  other arithmetic  51.3 us (3%)
  between operations  17.1 us (1%)
    gather x2, local copies, waits for them, and re-layouts, shards(): jnp.take(position_table.T, jnp.asarray(bucket_index), axis=1)  937 us
    reduce_scatter x1, waiting for transfers between devices, shards(): lax.psum_scatter(lax.dot_general(similarity_gradient, my_queries, (((0,),...  70.9 us
    unnamed x108, local copies, waits for them, and re-layouts  70.5 us
    rev x1, local copies, waits for them, and re-layouts, diagonal_sums(): flipped = square[:, :, ::-1]  64.2 us
    all_gather x1, blocking collectives, shards(): lax.all_gather(document_vectors, 'rows', axis=0, tiled=True)  45.4 us
    psum x1, blocking collectives, shards(): lax.psum((attention_gain_grad, query_grad, key_grad, value_grad, output_g...  37.9 us
    psum x1, waiting for transfers between devices, shards(): lax.psum((attention_gain_grad, query_grad, key_grad, value_grad, output_g...  32.4 us
  transfers between devices with their start and end apart: 5, of which 4 were waited for; matrix products, arithmetic and copies ran while one was open for 11% of the time, Pallas kernels for 0%

commit v1 on v0

--- a/solution.py
+++ b/solution.py
@@ -11,6 +11,12 @@
 SOFTMAX_TEMP = 0.01
 LOSS_SCALE = 65536.0
 MATMUL_PRECISION = lax.Precision.HIGHEST
+
+
+def laid_out(blocks, dim):
+    shape = list(blocks.shape[1:])
+    shape[dim] *= blocks.shape[0]
+    return jnp.moveaxis(blocks, 0, dim).reshape(shape)
 
 
 def from_partner(value, axis, apart):
@@ -177,7 +183,19 @@
     partner = from_partner(embedded_tokens, "tower", 0)
     query_vectors = jnp.where(is_query, embedded_tokens, partner)
     document_vectors = jnp.where(is_query, partner, embedded_tokens)
-    gathered_documents = lax.all_gather(document_vectors, "rows", axis=0, tiled=True)
+    size = lax.axis_size("rows")
+    pairs_2 = [(i, (i + 1) % size) for i in range(size)]
+    back = [(b, a) for a, b in pairs_2]
+    lower, upper = ([], [])
+    for step in range(size - 1):
+        if step % 2 == 0:
+            lower.append(lax.ppermute(lower[-1] if lower else document_vectors, "rows", pairs_2))
+        else:
+            upper.append(lax.ppermute(upper[-1] if upper else document_vectors, "rows", back))
+    blocks = jnp.stack([*lower[::-1], document_vectors, *upper])
+    shift = lax.axis_index("rows") - len(lower)
+    blocks = blocks[(jnp.arange(size) - shift) % size]
+    gathered_documents = laid_out(blocks, 0)
     item_total = gathered_documents.shape[0]
     half_items = items_here // 2
     my_queries = lax.dynamic_slice_in_dim(query_vectors, tower_index * half_items, half_items, 0)

time: 1500 us -> 1530 us (1.020)
  blocking collectives: 83.3 us -> 38 us
  starting transfers between devices: 0.76 us -> 42.4 us
  local copies, waits for them, and re-layouts: 1130 us -> 1150 us
  waiting for transfers between devices: 104 us -> 122 us
    all_gather x1 -> x0, blocking collectives: 45.4 us -> none  [shards(): lax.all_gather(document_vectors, 'rows', axis=0, tiled=True)]
    ppermute x0 -> x15, starting transfers between devices: none -> 41.6 us  [the longest x7 38.8 us: shards(): lax.ppermute(upper[-1] if upper else document_vectors, 'rows', back)]
    ppermute x0 -> x15, waiting for transfers between devices: none -> 18.1 us  [the longest x8 18.1 us: shards(): lax.ppermute(lower[-1] if lower else document_vectors, 'rows', pairs_2)]
    unnamed x108 -> x137, local copies, waits for them, and re-layouts: 70.5 us -> 83.5 us
  transfers between devices with their start and end apart: 5 -> 20, of which waited for: 4 -> 11; matrix products, arithmetic and copies ran while one was open for 11% -> 12% of each run, Pallas kernels for 0% -> 0%
where the time goes in v1:
time: 1530 us; the launch traced here: 1520 us
  local copies, waits for them, and re-layouts  1150 us (75%)
  waiting for transfers between devices  122 us (8%)
  matrix products  96.6 us (6%)
  other arithmetic  52.7 us (3%)
  starting transfers between devices  42.4 us (3%)
  blocking collectives  38 us (2%)
  between operations  17.1 us (1%)
    gather x2, local copies, waits for them, and re-layouts, shards(): jnp.take(position_table.T, jnp.asarray(bucket_index), axis=1)  937 us
    unnamed x137, local copies, waits for them, and re-layouts  83.5 us
    reduce_scatter x1, waiting for transfers between devices, shards(): lax.psum_scatter(lax.dot_general(similarity_gradient, my_queries, (((0,),...  70.8 us
    rev x1, local copies, waits for them, and re-layouts, diagonal_sums(): flipped = square[:, :, ::-1]  64.3 us
    ppermute x7, starting transfers between devices, shards(): lax.ppermute(upper[-1] if upper else document_vectors, 'rows', back)  38.8 us
    psum x1, blocking collectives, shards(): lax.psum((attention_gain_grad, query_grad, key_grad, value_grad, output_g...  38 us
    psum x1, waiting for transfers between devices, shards(): lax.psum((attention_gain_grad, query_grad, key_grad, value_grad, output_g...  32 us
  transfers between devices with their start and end apart: 20, of which 11 were waited for; matrix products, arithmetic and copies ran while one was open for 12% of the time, Pallas kernels for 0%

profile of v1, /device:TPU:0, one launch (start us, length us, event | category | flops | bytes accessed | tf_op | source)
XLA Modules:
  0.0 1519.9 jit_solution(14683131007279882732)
XLA Ops:
  26.5 865.9 %gather_fusion = f32[262144,8]{1,0:T(8,128)} fusion(f32[8,32]{0,1:T(8,128)S(1)} %bitcast.238, s32[262144]{0:T(1024)S(1)} %broadcast_clamp_fusion), kind=kCustom, calls=%fused_computation | custom fusion | bytes 17825792 | tf_op jit(solution)/shard_map/jit(_take)/gather | solution.py:116
  892.4 70.9 %copy.45 = f32[512,512,8]{0,1,2:T(8,128)} copy(f32[512,512,8]{2,1,0:T(8,128)} %bitcast.13) | data formatting | bytes 16777216 | tf_op jit(solution)/shard_map/jit(_take)/gather | solution.py:116
  964.4 22.9 %while.29 = (s32[]{:T(128)}, bf16[2,512,512]{2,1,0:T(8,128)(2,1)}, f32[2,8,512]{2,1,0:T(8,128)S(1)}, bf16[2,512,512]{1,2,0:T(8,128)(2,1)}, s32[2,512]{1,0:T(2,12...) while((s32[]{:T(128)}, bf16[2,512,512]{2,1,0:T(8,128)(2,1)}, ...), condition=%wide.region_4.5_spmd, body=%wide.region_1.0_spmd.sunk | while | flops 554168320 | bytes 41556588 | solution.py:150
  1002.4 5.9 collective-permute-done.1
  1008.3 5.6 collective-permute-start.9
  1015.8 5.6 collective-permute-start.10
  1023.4 5.6 collective-permute-start.11
  1038.4 5.6 collective-permute-start.13
  1046.2 5.7 collective-permute-start.14
  1054.9 5.6 collective-permute-start.15
  1083.1 70.8 %reduce-scatter.2.cloned.1.call-done = f32[16,512]{1,0:T(8,128)} async-done(((f32[256,512]{1,0:T(8,128)}), f32[16,512]{1,0:T(8,128)}) %reduce-scatter.2.cloned.1.call-update) | async-done | bytes 32784 | tf_op jit(solution)/shard_map/reduce_scatter | solution.py:226
  1184.1 74.4 %while.30 = (s32[]{:T(128)}, f32[8,512,512]{1,2,0:T(8,128)}, bf16[2,512,512]{2,1,0:T(8,128)(2,1)}, bf16[2,512,512]{2,1,0:T(8,128)(2,1)}, bf16[2,512,512]{2,1,0:T...) while((s32[]{:T(128)}, f32[8,512,512]{1,2,0:T(8,128)}, ...), condition=%wide.region_15.16_spmd.clone, body=%wide.region_13.15_spmd.clone.sunk | while | flops 1368387584 | bytes 197745472 | solution.py:297
  1197.3 9.8 select_add_fusion.2
  1232.9 13.0 select_add_fusion.2
  1271.9 64.3 %rev.6 = f32[8,512,512]{1,2,0:T(8,128)} reverse(f32[8,512,512]{1,2,0:T(8,128)} %get-tuple-element.126), dimensions={2} | reverse | bytes 16777216 | tf_op jit(solution)/shard_map/rev | solution.py:87
  1336.2 9.7 copy.71
  1345.9 11.6 pad_bitcast_fusion
  1357.5 15.4 %copy.73 = f32[1,8,512,1024]{3,1,2,0:T(8,128)S(1)} copy(f32[1,8,512,1024]{3,2,1,0:T(8,128)} %pad_bitcast_fusion) | data formatting | bytes 33554432
  1372.9 6.0 slice.16
  1378.9 13.0 reshape.469
  1391.9 17.6 %reshape.445 = f32[8,512,1023]{2,1,0:T(8,128)} reshape(f32[4190208]{0:T(1024)} %reshape.469) | data formatting | bytes 33521664 | tf_op jit(solution)/shard_map/reshape | solution.py:90
  1409.5 7.4 reduce_sum.180
  1422.9 38.0 %all-reduce.1 = (f32[512]{0:T(512)}, f32[32,8]{0,1:T(8,128)}, f32[512]{0:T(512)}, f32[1]{0:T(128)}, f32[4]{0:T(128)S(1)}) all-reduce(f32[512]{0:T(512)S(1)} %get-tuple-element.208, f32[32,8]{0,1:T(8,128)S(1)} %fusion.50, f32[512]{0:T(512)S(1)} %copy-done.53, f32[1]{0:T(128)} %bitcast.45, ...), channel_id=1, replica_groups=mesh['tower'=2,'rows'=16] {'tower','rows'}, use_global_device_ids=true, to_apply=%region_18.19 | all-reduce | flops 1285 | bytes 10280 | tf_op jit(solution)/shard_map/psum | solution.py:320
  1467.4 32.0 %all-reduce.5.cloned.1.call-done = (f32[512,512]{1,0:T(8,128)}, f32[512,512]{1,0:T(8,128)}, f32[512,512]{1,0:T(8,128)}, f32[512,512]{1,0:T(8,128)}, f32[512,2048]{1,0:T(8,128)}, /*index=5*/f32[2048,512]{1,0:T(8,128)}) async-done(((f32[512,512]{1,0:T(8,128)}, f32[512,512]{1,0:T(8,128)}, f32[512,512]{1,0:T(8,128)}, f32[512,512]{1,0:T(8,128)}, f32[512,2048]{1,0:T(8,128)}, /*index=5*/f32[2048,512]{1,0:T(8,128)}), ...) | async-done | bytes 12582928 | tf_op jit(solution)/shard_map/psum | solution.py:320
  (305 shorter events, 217.1 us)
Async XLA Ops:
  7.2 982.7 %copy-start = (bf16[512,2048]{1,0:T(8,128)(2,1)S(1)}, bf16[512,2048]{1,0:T(8,128)(2,1)}, u32[]{:S(2)}) copy-start(bf16[512,2048]{1,0:T(8,128)(2,1)} %param.28) | copy-start | bytes 6291460
  7.2 1146.8 %reduce-scatter.2.cloned.1.call-start = ((), (), s32[]{:S(2)}) async-start(), calls=%async_computation.1 | async-start | bytes 557056 | tf_op jit(solution)/shard_map/reduce_scatter | solution.py:226
  998.2 1.3 collective-permute-start
  999.6 8.7 collective-permute-start.1
  1008.3 7.5 collective-permute-start.2
  1008.3 7.5 collective-permute-start.9
  1015.8 7.5 collective-permute-start.3
  1015.8 7.5 collective-permute-start.10
  1023.3 7.5 collective-permute-start.4
  1023.4 7.5 collective-permute-start.11
  1030.9 7.5 collective-permute-start.5
  1031.5 6.9 collective-permute-start.12
  1038.4 7.8 collective-permute-start.6
  1038.4 7.8 collective-permute-start.13
  1046.1 7.5 collective-permute-start.7
  1046.2 8.7 collective-permute-start.14
  1053.7 7.5 collective-permute-start.8
  1054.9 19.5 %collective-permute-start.15 = (f32[16,512]{1,0:T(8,128)}, f32[16,512]{1,0:T(8,128)S(1)}, u32[]{:S(2)}, u32[]{:S(2)}) collective-permute-start(f32[16,512]{1,0:T(8,128)} %collective-permute-done.14), channel_id=1, source_target_pairs={{1,0},{2,1},{3,2},{4,3},{5,4},{6,5},{7,6},{8,7},{9,8},{10,9},{11,1... | collective-permute-start | bytes 98312 | tf_op jit(solution)/shard_map/ppermute | solution.py:194
  1062.4 91.6 %copy-start.5 = (bf16[1,2,512,512]{3,2,1,0:T(8,128)(2,1)S(1)}, bf16[1,2,512,512]{3,2,1,0:T(8,128)(2,1)}, u32[]{:S(2)}) copy-start(bf16[1,2,512,512]{3,2,1,0:T(8,128)(2,1)} %param.18) | copy-start | bytes 3145732
  1062.4 91.6 %copy-start.34 = (f32[512]{0:T(512)S(1)}, f32[512]{0:T(512)}, u32[]{:S(2)}) copy-start(f32[512]{0:T(512)} %param.21) | copy-start | bytes 6148
  1077.5 78.5 %copy-start.43 = (f32[16]{0:T(128)S(1)}, f32[16]{0:T(128)}, u32[]{:S(2)}) copy-start(f32[16]{0:T(128)} %copy-done.42) | copy-start | bytes 196
  1081.4 418.0 %all-reduce.5.cloned.1.call-start = ((), (), s32[]{:S(2)}) async-start(), calls=%async_computation.2 | async-start | bytes 25165824 | tf_op jit(solution)/shard_map/psum | solution.py:320
  1083.1 72.8 %collective-permute-start.16 = (f32[8,512]{1,0:T(8,128)S(1)}, f32[8,512]{1,0:T(8,128)S(1)}, u32[]{:S(2)}, u32[]{:S(2)}) collective-permute-start(f32[8,512]{1,0:T(8,128)S(1)} %convolution_multiply_fusion.1), channel_id=1, source_target_pairs={{0,16},{16,0},{1,17},{17,1},{2,18},{18,2},{3,19},{19,3},{4,20},{20... | collective-permute-start | bytes 49160 | tf_op jit(solution)/shard_map/ppermute | solution.py:25
  1154.0 2.0 collective-permute-start.17
  (60 other events, 546.4 us)
Sparse Core Ops, SparseCore 0:
  1081.6 72.3 reduce-scatter.1
  1265.5 233.8 all-reduce.4
